TPU v7x, 32 devices: a whole 2x2x4 slice. The times are simulated.
32 devices in a mesh: rows: 8 (over z, x), gate: 4 (over y, core).
Axes of the slice: x: 2, y: 2, z: 4, core: 2. Of those that a mesh axis runs over, the one named last changes fastest.
Arguments:
- frames: bfloat16 [8, 8, 16, 16, 128], P(None, None, None, 'rows'), may hold values from -6 to 6
- validity: int32 [8, 16, 128], P(None, 'rows'), may hold values 0 or 1
- encoding_start_hidden: bfloat16 [8, 128, 16, 128], P(None, 'gate', 'rows'), may hold values from -3 to 3
- encoding_start_cell: float32 [8, 128, 16, 128], P(None, 'gate', 'rows'), may hold values from -3 to 3
- encoding_input_kernel: bfloat16 [4, 128, 9, 16], P(None, 'gate'), may hold values from -0.5 to 0.5
- encoding_recurrent_kernel: bfloat16 [4, 128, 9, 128], P(None, 'gate'), may hold values from -0.1875 to 0.1875
- encoding_gate_bias: float32 [4, 128], P(None, 'gate'), may hold values from -3 to 3
- encoding_peephole_weight: float32 [3, 128], P(None, 'gate'), may hold values from -3 to 3
- predicting_start_hidden: bfloat16 [8, 128, 16, 128], P(None, 'gate', 'rows'), may hold values from -3 to 3
- predicting_start_cell: float32 [8, 128, 16, 128], P(None, 'gate', 'rows'), may hold values from -3 to 3
- predicting_input_kernel: bfloat16 [4, 128, 9, 128], P(None, 'gate'), may hold values from -0.1875 to 0.1875
- predicting_recurrent_kernel: bfloat16 [4, 128, 9, 128], P(None, 'gate'), may hold values from -0.1875 to 0.1875
- predicting_gate_bias: float32 [4, 128], P(None, 'gate'), may hold values from -3 to 3
- predicting_peephole_weight: float32 [3, 128], P(None, 'gate'), may hold values from -3 to 3
- cotangent: bfloat16 [8, 8, 128, 16, 128], P(None, None, 'gate', 'rows'), may hold values from -6 to 6
Outputs:
- predicted: bfloat16 [8, 8, 128, 16, 128], P(None, None, 'gate', 'rows')
- frames_gradient: float32 [8, 8, 16, 16, 128], P(None, None, 'gate', 'rows')
- encoder_hidden_gradient: float32 [8, 128, 16, 128], P(None, 'gate', 'rows')
- encoder_cell_gradient: float32 [8, 128, 16, 128], P(None, 'gate', 'rows')
- encoder_kernel_gradient: float32 [4, 128, 9, 16], P(None, 'gate')
- encoder_recurrent_gradient: float32 [4, 128, 9, 128], P(None, 'gate')
- encoder_bias_gradient: float32 [4, 128], P(None, 'gate')
- encoder_peephole_gradient: float32 [3, 128], P(None, 'gate')
- forecast_hidden_gradient: float32 [8, 128, 16, 128], P(None, 'gate', 'rows')
- forecast_cell_gradient: float32 [8, 128, 16, 128], P(None, 'gate', 'rows')
- forecast_kernel_gradient: float32 [4, 128, 9, 128], P(None, 'gate')
- forecast_recurrent_gradient: float32 [4, 128, 9, 128], P(None, 'gate')
- forecast_bias_gradient: float32 [4, 128], P(None, 'gate')
- forecast_peephole_gradient: float32 [3, 128], P(None, 'gate')
All inputs are finite; a program needn't handle non-finite values. No bound on the sum of `validity` on one device may be relied on, other than what follows from the above.
Results may differ from a plain program's by a relative error of at most 0.006.
Values may be sent and summed in bfloat16 or wider, within the bound.
No kernel may reach another device: no remote copies, remote signals or barrier semaphores. Data moves between devices by JAX's collectives and lax.ppermute only.
A program may use at most 192 MiB of HBM per device.

v0:
```python
import jax
import jax.numpy as jnp
from jax import lax
from jax.sharding import PartitionSpec as P


def extended(value, sides, width):
    for axis, dim in sides:
        devices, length = (lax.axis_size(axis), value.shape[dim])
        up = [(i, (i + 1) % devices) for i in range(devices - 1)]
        down = [(j, i) for i, j in up]
        last = lax.slice_in_dim(value, length - width, length, axis=dim)
        leading = lax.slice_in_dim(value, 0, width, axis=dim)
        before = lax.ppermute(last, axis, up)
        after = lax.ppermute(leading, axis, down)
        value = jnp.concatenate([before, value, after], axis=dim)
    return value


def shift_columns(values, delta):
    if delta == 0:
        return values
    widths = ((0, 0), (0, 0), (0, 0))
    if delta > 0:
        return jnp.pad(values[:, :, :, delta:], widths + ((0, delta),))
    return jnp.pad(values[:, :, :, :delta], widths + ((-delta, 0),))


def apply_taps(padded, taps, reverse):
    own_rows = padded.shape[2] - 2
    total = None
    for col_off in range(3):
        partial_sum = None
        for row_off in range(3):
            first_row = 2 - row_off if reverse else row_off
            term = jnp.einsum(
                "oc,ncyx->noyx",
                taps[3 * row_off + col_off],
                padded[:, :, first_row : first_row + own_rows, :],
                preferred_element_type=jnp.float32,
            )
            partial_sum = term if partial_sum is None else partial_sum + term
        moved = shift_columns(partial_sum, 1 - col_off if reverse else col_off - 1)
        total = moved if total is None else total + moved
    return total


def forward_taps(kernel):
    outputs = kernel.shape[0] * kernel.shape[1]
    return kernel.reshape(outputs, 9, kernel.shape[3]).transpose(1, 0, 2)


def arrange(kernel):
    outputs = kernel.shape[0] * kernel.shape[1]
    return kernel.reshape(outputs, 9, kernel.shape[3]).transpose(1, 2, 0)


def weight_terms(rounded, padded):
    own_rows = padded.shape[2] - 2
    results = [None] * 9
    for col_off in range(3):
        shifted = shift_columns(padded, col_off - 1)
        for row_off in range(3):
            results[3 * row_off + col_off] = jnp.einsum(
                "noyx,ncyx->oc",
                rounded,
                shifted[:, :, row_off : row_off + own_rows, :],
                preferred_element_type=jnp.float32,
            )
    return jnp.stack(results, axis=1)


def spread(hidden_now):
    gathered = lax.all_gather(hidden_now, "gate", axis=1, tiled=True)
    return extended(gathered, (("rows", 2),), 1)


def gate_math(gate_values, stored, peephole):
    inflow = jax.nn.sigmoid(gate_values[:, 0] + peephole[0][None, :, None] * stored)
    forget = jax.nn.sigmoid(gate_values[:, 1] + peephole[1][None, :, None] * stored)
    candidate = jnp.tanh(gate_values[:, 3])
    renewed = forget * stored + inflow * candidate
    outflow = jax.nn.sigmoid(gate_values[:, 2] + peephole[2][None, :, None] * renewed)
    return (inflow, forget, candidate, renewed, outflow)


def layer_forward_pass(
    inputs_padded, hidden_start, memory_start, kernel, recurrent, bias, peephole
):
    images, own_channels, own_rows, across = hidden_start.shape
    pixels = own_rows * across
    input_taps = forward_taps(kernel)
    hidden_taps = forward_taps(recurrent)

    def advance(carried, current):
        hidden_now, stored = carried
        beside_all = spread(hidden_now)
        gate_values = apply_taps(current, input_taps, False) + apply_taps(
            beside_all, hidden_taps, False
        )
        gate_values = gate_values.reshape(images, 4, own_channels, pixels) + bias[None, :, :, None]
        inflow, forget, candidate, renewed, outflow = gate_math(gate_values, stored, peephole)
        emitted = (
            (outflow * jnp.tanh(renewed))
            .astype(jnp.bfloat16)
            .reshape(images, own_channels, own_rows, across)
        )
        return ((emitted, renewed), (beside_all, gate_values, stored, emitted))

    start_state = (hidden_start, memory_start.reshape(images, own_channels, pixels))
    final_state, kept = lax.scan(advance, start_state, inputs_padded)
    return (final_state[0], kept)


def layer_backward_pass(inputs_padded, kept, incoming, kernel, recurrent, peephole):
    arounds, gate_all, memories, emitted_all = kept
    images, fours, own_channels, pixels = gate_all.shape[1:]
    own_rows = inputs_padded.shape[3] - 2
    across = inputs_padded.shape[4]
    back_kernel = arrange(kernel)
    back_recurrent = arrange(recurrent)
    zero_state = jnp.zeros((images, own_channels, pixels), jnp.float32)
    start_sums = (
        zero_state,
        zero_state,
        jnp.zeros((4 * own_channels, 9, kernel.shape[3]), jnp.float32),
        jnp.zeros((4 * own_channels, 9, recurrent.shape[3]), jnp.float32),
        jnp.zeros((4, own_channels), jnp.float32),
        jnp.zeros((3, own_channels), jnp.float32),
    )

    def retreat(carried, slices):
        grad_hidden, grad_memory, sum_kernel, sum_recurrent, sum_bias, sum_peephole = carried
        current, beside_all, gate_values, stored, outside = slices
        inflow, forget, candidate, renewed, outflow = gate_math(gate_values, stored, peephole)
        squashed = jnp.tanh(renewed)
        hidden_total = outside + grad_hidden
        grad_outflow = hidden_total * squashed * outflow * (1.0 - outflow)
        grad_renewed = (
            grad_memory
            + hidden_total * outflow * (1.0 - squashed * squashed)
            + grad_outflow * peephole[2][None, :, None]
        )
        grad_inflow = grad_renewed * candidate * inflow * (1.0 - inflow)
        grad_forget = grad_renewed * stored * forget * (1.0 - forget)
        grad_candidate = grad_renewed * inflow * (1.0 - candidate * candidate)
        grad_stored = (
            grad_renewed * forget
            + grad_inflow * peephole[0][None, :, None]
            + grad_forget * peephole[1][None, :, None]
        )
        grad_gates = jnp.stack([grad_inflow, grad_forget, grad_outflow, grad_candidate], axis=1)
        sum_bias = sum_bias + jnp.sum(grad_gates, axis=(0, 3))
        sum_peephole = sum_peephole + jnp.stack(
            [
                jnp.sum(grad_inflow * stored, axis=(0, 2)),
                jnp.sum(grad_forget * stored, axis=(0, 2)),
                jnp.sum(grad_outflow * renewed, axis=(0, 2)),
            ]
        )
        rounded = grad_gates.reshape(images, 4 * own_channels, own_rows, across).astype(
            jnp.bfloat16
        )
        padded = extended(rounded, (("rows", 2),), 1)
        toward_hidden = apply_taps(padded, back_recurrent, True)
        toward_input = apply_taps(padded, back_kernel, True)
        hidden_back, input_back = (
            lax.psum_scatter(toward_hidden, "gate", scatter_dimension=1, tiled=True),
            lax.psum_scatter(toward_input, "gate", scatter_dimension=1, tiled=True),
        )
        sum_kernel = sum_kernel + weight_terms(rounded, current)
        sum_recurrent = sum_recurrent + weight_terms(rounded, beside_all)
        hidden_back = hidden_back.reshape(images, hidden_back.shape[1], pixels)
        input_back = input_back.reshape(images, input_back.shape[1], pixels)
        return (
            (hidden_back, grad_stored, sum_kernel, sum_recurrent, sum_bias, sum_peephole),
            input_back,
        )

    final_sums, input_grads = lax.scan(
        retreat, start_sums, (inputs_padded, arounds, gate_all, memories, incoming), reverse=True
    )
    return (final_sums, input_grads)


def per_device(
    frames,
    validity,
    encoding_start_hidden,
    encoding_start_cell,
    encoding_input_kernel,
    encoding_recurrent_kernel,
    encoding_gate_bias,
    encoding_peephole_weight,
    predicting_start_hidden,
    predicting_start_cell,
    predicting_input_kernel,
    predicting_recurrent_kernel,
    predicting_gate_bias,
    predicting_peephole_weight,
    cotangent,
):
    valid_low = validity.astype(jnp.bfloat16)
    valid_full = validity.astype(jnp.float32)
    masked = frames * valid_low[None, :, None, :, :]
    padded_frames = extended(masked, (("rows", 3),), 1)
    encoder_end, encoding_saved_states = layer_forward_pass(
        padded_frames,
        encoding_start_hidden,
        encoding_start_cell,
        encoding_input_kernel,
        encoding_recurrent_kernel,
        encoding_gate_bias,
        encoding_peephole_weight,
    )
    closing_wrapper = spread(encoder_end)
    predicting_input_frames = jnp.concatenate(
        [encoding_saved_states[0][1:], closing_wrapper[None]], axis=0
    )
    predicting_last_state, predicting_saved_states = layer_forward_pass(
        predicting_input_frames,
        predicting_start_hidden,
        predicting_start_cell,
        predicting_input_kernel,
        predicting_recurrent_kernel,
        predicting_gate_bias,
        predicting_peephole_weight,
    )
    predicted = predicting_saved_states[3]
    frames_count, images, own_channels, own_rows, across = cotangent.shape
    incoming = (cotangent.astype(jnp.float32) * valid_full[None, :, None, :, :]).reshape(
        frames_count, images, own_channels, own_rows * across
    )
    predicting_gradient_sums, gradient_into_encoding = layer_backward_pass(
        predicting_input_frames,
        predicting_saved_states,
        incoming,
        predicting_input_kernel,
        predicting_recurrent_kernel,
        predicting_peephole_weight,
    )
    encoder_sums, toward_frames = layer_backward_pass(
        padded_frames,
        encoding_saved_states,
        gradient_into_encoding,
        encoding_input_kernel,
        encoding_recurrent_kernel,
        encoding_peephole_weight,
    )
    frames_gradient = (
        toward_frames.reshape(frames_count, images, toward_frames.shape[2], own_rows, across)
        * valid_full[None, :, None, :, :]
    )
    running_sums = lax.psum(
        (
            encoder_sums[2],
            encoder_sums[3],
            encoder_sums[4],
            encoder_sums[5],
            predicting_gradient_sums[2],
            predicting_gradient_sums[3],
            predicting_gradient_sums[4],
            predicting_gradient_sums[5],
        ),
        "rows",
    )
    state_dimensions = (images, own_channels, own_rows, across)
    return (
        predicted,
        frames_gradient,
        encoder_sums[0].reshape(state_dimensions),
        encoder_sums[1].reshape(state_dimensions),
        running_sums[0].reshape(encoding_input_kernel.shape),
        running_sums[1].reshape(encoding_recurrent_kernel.shape),
        running_sums[2],
        running_sums[3],
        predicting_gradient_sums[0].reshape(state_dimensions),
        predicting_gradient_sums[1].reshape(state_dimensions),
        running_sums[4].reshape(predicting_input_kernel.shape),
        running_sums[5].reshape(predicting_recurrent_kernel.shape),
        running_sums[6],
        running_sums[7],
    )


def solution(mesh):
    return jax.shard_map(
        per_device,
        mesh=mesh,
        in_specs=(
            P(None, None, None, "rows", None),
            P(None, "rows", None),
            P(None, "gate", "rows", None),
            P(None, "gate", "rows", None),
            P(None, "gate", None, None),
            P(None, "gate", None, None),
            P(None, "gate"),
            P(None, "gate"),
            P(None, "gate", "rows", None),
            P(None, "gate", "rows", None),
            P(None, "gate", None, None),
            P(None, "gate", None, None),
            P(None, "gate"),
            P(None, "gate"),
            P(None, None, "gate", "rows", None),
        ),
        out_specs=(
            P(None, None, "gate", "rows", None),
            P(None, None, "gate", "rows", None),
            P(None, "gate", "rows", None),
            P(None, "gate", "rows", None),
            P(None, "gate", None, None),
            P(None, "gate", None, None),
            P(None, "gate"),
            P(None, "gate"),
            P(None, "gate", "rows", None),
            P(None, "gate", "rows", None),
            P(None, "gate", None, None),
            P(None, "gate", None, None),
            P(None, "gate"),
            P(None, "gate"),
        ),
        check_vma=False,
    )
```

profile of v0, /device:TPU:0, one launch (start us, length us, event | category | flops | bytes accessed | tf_op | source)
XLA Modules:
  0.0 2376.9 jit_solution(14796101239716344886)
XLA Ops:
  33.3 337.4 %while.96 = (s32[]{:T(128)}, bf16[8,32,2,128]{3,2,1,0:T(2,128)(2,1)S(1)}, f32[8,32,256]{2,1,0:T(8,128)}, bf16[8,8,128,4,128]{4,2,3,1,0:T(8,128)(2,1)}, f32[8,8,4...) while((s32[]{:T(128)}, ...), condition=%wide.region_1.2_spmd, body=%wide.region_0.1_spmd.sunk | while | flops 696254464 | bytes 89053784 | solution.py:111
  381.6 11.9 collective-permute-start.11
  402.6 9.2 slice.1493
  425.0 387.1 %while.97 = (s32[]{:T(128)}, bf16[8,32,2,128]{3,2,1,0:T(2,128)(2,1)S(1)}, f32[8,32,256]{2,1,0:T(8,128)}, bf16[8,8,128,4,128]{4,1,3,2,0:T(8,128)(2,1)}, f32[8,8,4...) while((s32[]{:T(128)}, ...), condition=%wide.region_3.4_spmd, body=%wide.region_2.3_spmd.sunk | while | flops 1226833920 | bytes 117983880 | solution.py:111
  814.4 718.4 %while.98 = (s32[]{:T(128)}, f32[8,32,256]{2,1,0:T(8,128)}, f32[8,32,256]{2,1,0:T(8,128)}, f32[128,9,128]{2,0,1:T(8,128)}, f32[128,9,128]{2,0,1:T(8,128)}, /*ind...) while((s32[]{:T(128)}, f32[8,32,256]{2,1,0:T(8,128)}, ...), condition=%wide.region_11.12_spmd.clone, body=%wide.region_4.11_spmd.clone.sunk | while | flops 2445541888 | bytes 173979664 | solution.py:180
  864.5 10.1 reduce-scatter.7.cloned.1.call-done
  875.9 26.3 %reduce-scatter.5.cloned.1.call-done = f32[8,32,2,128]{3,0,2,1:T(8,128)} async-done(((f32[8,128,2,128]{3,0,2,1:T(8,128)}), f32[8,32,2,128]{3,0,2,1:T(8,128)}) %reduce-scatter.5.cloned.1.call-update) | async-done | bytes 262160 | tf_op jit(solution)/shard_map/while/body/eval_jaxpr/reduce_scatter | solution.py:168
  954.0 10.4 reduce-scatter.7.cloned.1.call-done
  965.7 26.1 %reduce-scatter.5.cloned.1.call-done = f32[8,32,2,128]{3,0,2,1:T(8,128)} async-done(((f32[8,128,2,128]{3,0,2,1:T(8,128)}), f32[8,32,2,128]{3,0,2,1:T(8,128)}) %reduce-scatter.5.cloned.1.call-update) | async-done | bytes 262160 | tf_op jit(solution)/shard_map/while/body/eval_jaxpr/reduce_scatter | solution.py:168
  1043.6 10.4 reduce-scatter.7.cloned.1.call-done
  1055.3 26.2 %reduce-scatter.5.cloned.1.call-done = f32[8,32,2,128]{3,0,2,1:T(8,128)} async-done(((f32[8,128,2,128]{3,0,2,1:T(8,128)}), f32[8,32,2,128]{3,0,2,1:T(8,128)}) %reduce-scatter.5.cloned.1.call-update) | async-done | bytes 262160 | tf_op jit(solution)/shard_map/while/body/eval_jaxpr/reduce_scatter | solution.py:168
  1133.3 10.4 reduce-scatter.7.cloned.1.call-done
  1145.0 26.3 %reduce-scatter.5.cloned.1.call-done = f32[8,32,2,128]{3,0,2,1:T(8,128)} async-done(((f32[8,128,2,128]{3,0,2,1:T(8,128)}), f32[8,32,2,128]{3,0,2,1:T(8,128)}) %reduce-scatter.5.cloned.1.call-update) | async-done | bytes 262160 | tf_op jit(solution)/shard_map/while/body/eval_jaxpr/reduce_scatter | solution.py:168
  1223.1 10.4 reduce-scatter.7.cloned.1.call-done
  1234.8 26.1 %reduce-scatter.5.cloned.1.call-done = f32[8,32,2,128]{3,0,2,1:T(8,128)} async-done(((f32[8,128,2,128]{3,0,2,1:T(8,128)}), f32[8,32,2,128]{3,0,2,1:T(8,128)}) %reduce-scatter.5.cloned.1.call-update) | async-done | bytes 262160 | tf_op jit(solution)/shard_map/while/body/eval_jaxpr/reduce_scatter | solution.py:168
  1312.7 10.4 reduce-scatter.7.cloned.1.call-done
  1324.4 26.1 %reduce-scatter.5.cloned.1.call-done = f32[8,32,2,128]{3,0,2,1:T(8,128)} async-done(((f32[8,128,2,128]{3,0,2,1:T(8,128)}), f32[8,32,2,128]{3,0,2,1:T(8,128)}) %reduce-scatter.5.cloned.1.call-update) | async-done | bytes 262160 | tf_op jit(solution)/shard_map/while/body/eval_jaxpr/reduce_scatter | solution.py:168
  1402.3 10.4 reduce-scatter.7.cloned.1.call-done
  1414.1 26.2 %reduce-scatter.5.cloned.1.call-done = f32[8,32,2,128]{3,0,2,1:T(8,128)} async-done(((f32[8,128,2,128]{3,0,2,1:T(8,128)}), f32[8,32,2,128]{3,0,2,1:T(8,128)}) %reduce-scatter.5.cloned.1.call-update) | async-done | bytes 262160 | tf_op jit(solution)/shard_map/while/body/eval_jaxpr/reduce_scatter | solution.py:168
  1492.0 10.4 reduce-scatter.7.cloned.1.call-done
  1503.7 26.2 %reduce-scatter.5.cloned.1.call-done = f32[8,32,2,128]{3,0,2,1:T(8,128)} async-done(((f32[8,128,2,128]{3,0,2,1:T(8,128)}), f32[8,32,2,128]{3,0,2,1:T(8,128)}) %reduce-scatter.5.cloned.1.call-update) | async-done | bytes 262160 | tf_op jit(solution)/shard_map/while/body/eval_jaxpr/reduce_scatter | solution.py:168
  1534.3 722.4 %while.99 = (s32[]{:T(128)}, f32[8,32,256]{2,1,0:T(8,128)}, f32[8,32,256]{2,1,0:T(8,128)}, f32[128,9,16]{0,2,1:T(8,128)}, f32[128,9,128]{2,0,1:T(8,128)}, /*inde...) while((s32[]{:T(128)}, f32[8,32,256]{2,1,0:T(8,128)}, ...), condition=%wide.region_19.20_spmd.clone, body=%wide.region_12.19_spmd.clone.sunk | while | flops 1386484096 | bytes 121870768 | solution.py:180
  1595.7 26.1 %reduce-scatter.9.cloned.1.call-done = f32[8,32,2,128]{3,0,2,1:T(8,128)} async-done(((f32[8,128,2,128]{3,0,2,1:T(8,128)}), f32[8,32,2,128]{3,0,2,1:T(8,128)}) %reduce-scatter.9.cloned.1.call-update) | async-done | bytes 262160 | tf_op jit(solution)/shard_map/while/body/eval_jaxpr/reduce_scatter | solution.py:168
  1686.0 26.1 %reduce-scatter.9.cloned.1.call-done = f32[8,32,2,128]{3,0,2,1:T(8,128)} async-done(((f32[8,128,2,128]{3,0,2,1:T(8,128)}), f32[8,32,2,128]{3,0,2,1:T(8,128)}) %reduce-scatter.9.cloned.1.call-update) | async-done | bytes 262160 | tf_op jit(solution)/shard_map/while/body/eval_jaxpr/reduce_scatter | solution.py:168
  1776.4 26.2 %reduce-scatter.9.cloned.1.call-done = f32[8,32,2,128]{3,0,2,1:T(8,128)} async-done(((f32[8,128,2,128]{3,0,2,1:T(8,128)}), f32[8,32,2,128]{3,0,2,1:T(8,128)}) %reduce-scatter.9.cloned.1.call-update) | async-done | bytes 262160 | tf_op jit(solution)/shard_map/while/body/eval_jaxpr/reduce_scatter | solution.py:168
  1866.9 26.1 %reduce-scatter.9.cloned.1.call-done = f32[8,32,2,128]{3,0,2,1:T(8,128)} async-done(((f32[8,128,2,128]{3,0,2,1:T(8,128)}), f32[8,32,2,128]{3,0,2,1:T(8,128)}) %reduce-scatter.9.cloned.1.call-update) | async-done | bytes 262160 | tf_op jit(solution)/shard_map/while/body/eval_jaxpr/reduce_scatter | solution.py:168
  1957.3 26.1 %reduce-scatter.9.cloned.1.call-done = f32[8,32,2,128]{3,0,2,1:T(8,128)} async-done(((f32[8,128,2,128]{3,0,2,1:T(8,128)}), f32[8,32,2,128]{3,0,2,1:T(8,128)}) %reduce-scatter.9.cloned.1.call-update) | async-done | bytes 262160 | tf_op jit(solution)/shard_map/while/body/eval_jaxpr/reduce_scatter | solution.py:168
  2047.6 26.2 %reduce-scatter.9.cloned.1.call-done = f32[8,32,2,128]{3,0,2,1:T(8,128)} async-done(((f32[8,128,2,128]{3,0,2,1:T(8,128)}), f32[8,32,2,128]{3,0,2,1:T(8,128)}) %reduce-scatter.9.cloned.1.call-update) | async-done | bytes 262160 | tf_op jit(solution)/shard_map/while/body/eval_jaxpr/reduce_scatter | solution.py:168
  2138.1 26.1 %reduce-scatter.9.cloned.1.call-done = f32[8,32,2,128]{3,0,2,1:T(8,128)} async-done(((f32[8,128,2,128]{3,0,2,1:T(8,128)}), f32[8,32,2,128]{3,0,2,1:T(8,128)}) %reduce-scatter.9.cloned.1.call-update) | async-done | bytes 262160 | tf_op jit(solution)/shard_map/while/body/eval_jaxpr/reduce_scatter | solution.py:168
  2228.4 26.2 %reduce-scatter.9.cloned.1.call-done = f32[8,32,2,128]{3,0,2,1:T(8,128)} async-done(((f32[8,128,2,128]{3,0,2,1:T(8,128)}), f32[8,32,2,128]{3,0,2,1:T(8,128)}) %reduce-scatter.9.cloned.1.call-update) | async-done | bytes 262160 | tf_op jit(solution)/shard_map/while/body/eval_jaxpr/reduce_scatter | solution.py:168
  2264.9 23.4 all-reduce.24
  2289.1 76.0 %all-reduce.28.cloned.1.call-done = (f32[4,32,9,16]{1,0,3,2:T(4,128)}, f32[4,32,9,128]{3,1,0,2:T(8,128)}, f32[4,32,9,128]{3,1,0,2:T(8,128)}, f32[4,32,9,128]{3,1,0,2:T(8,128)}) async-done(((f32[4,32,9,16]{1,0,3,2:T(4,128)}, f32[4,32,9,128]{3,1,0,2:T(8,128)}, f32[4,32,9,128]{3,1,0,2:T(8,128)}, f32[4,32,9,128]{3,1,0,2:T(8,128)}), (f32[4,32,9,16]{1,0,3,2:T(4,128)}, f32[4,32,9,128]{3,1,0,2:T(8,128)}, ...) | async-done | bytes 1843216 | tf_op jit(solution)/shard_map/psum | solution.py:254
  (2850 shorter events, 1727.5 us)
Async XLA Ops:
  814.8 59.8 %reduce-scatter.7.cloned.1.call-start = ((), (), s32[]{:S(2)}) async-start(), calls=%async_computation.6 | async-start | bytes 1310720 | tf_op jit(solution)/shard_map/while/body/eval_jaxpr/reduce_scatter | solution.py:169
  848.7 53.6 %reduce-scatter.5.cloned.1.call-start = ((), (), s32[]{:S(2)}) async-start(), calls=%async_computation.5 | async-start | bytes 1310720 | tf_op jit(solution)/shard_map/while/body/eval_jaxpr/reduce_scatter | solution.py:168
  905.0 59.5 %reduce-scatter.7.cloned.1.call-start = ((), (), s32[]{:S(2)}) async-start(), calls=%async_computation.6 | async-start | bytes 1310720 | tf_op jit(solution)/shard_map/while/body/eval_jaxpr/reduce_scatter | solution.py:169
  938.2 53.7 %reduce-scatter.5.cloned.1.call-start = ((), (), s32[]{:S(2)}) async-start(), calls=%async_computation.5 | async-start | bytes 1310720 | tf_op jit(solution)/shard_map/while/body/eval_jaxpr/reduce_scatter | solution.py:168
  994.6 59.4 %reduce-scatter.7.cloned.1.call-start = ((), (), s32[]{:S(2)}) async-start(), calls=%async_computation.6 | async-start | bytes 1310720 | tf_op jit(solution)/shard_map/while/body/eval_jaxpr/reduce_scatter | solution.py:169
  1027.8 53.7 %reduce-scatter.5.cloned.1.call-start = ((), (), s32[]{:S(2)}) async-start(), calls=%async_computation.5 | async-start | bytes 1310720 | tf_op jit(solution)/shard_map/while/body/eval_jaxpr/reduce_scatter | solution.py:168
  1084.3 59.4 %reduce-scatter.7.cloned.1.call-start = ((), (), s32[]{:S(2)}) async-start(), calls=%async_computation.6 | async-start | bytes 1310720 | tf_op jit(solution)/shard_map/while/body/eval_jaxpr/reduce_scatter | solution.py:169
  1117.4 53.9 %reduce-scatter.5.cloned.1.call-start = ((), (), s32[]{:S(2)}) async-start(), calls=%async_computation.5 | async-start | bytes 1310720 | tf_op jit(solution)/shard_map/while/body/eval_jaxpr/reduce_scatter | solution.py:168
  1174.0 59.5 %reduce-scatter.7.cloned.1.call-start = ((), (), s32[]{:S(2)}) async-start(), calls=%async_computation.6 | async-start | bytes 1310720 | tf_op jit(solution)/shard_map/while/body/eval_jaxpr/reduce_scatter | solution.py:169
  1207.3 53.7 %reduce-scatter.5.cloned.1.call-start = ((), (), s32[]{:S(2)}) async-start(), calls=%async_computation.5 | async-start | bytes 1310720 | tf_op jit(solution)/shard_map/while/body/eval_jaxpr/reduce_scatter | solution.py:168
  1263.7 59.4 %reduce-scatter.7.cloned.1.call-start = ((), (), s32[]{:S(2)}) async-start(), calls=%async_computation.6 | async-start | bytes 1310720 | tf_op jit(solution)/shard_map/while/body/eval_jaxpr/reduce_scatter | solution.py:169
  1296.9 53.7 %reduce-scatter.5.cloned.1.call-start = ((), (), s32[]{:S(2)}) async-start(), calls=%async_computation.5 | async-start | bytes 1310720 | tf_op jit(solution)/shard_map/while/body/eval_jaxpr/reduce_scatter | solution.py:168
  1353.3 59.5 %reduce-scatter.7.cloned.1.call-start = ((), (), s32[]{:S(2)}) async-start(), calls=%async_computation.6 | async-start | bytes 1310720 | tf_op jit(solution)/shard_map/while/body/eval_jaxpr/reduce_scatter | solution.py:169
  1386.5 53.8 %reduce-scatter.5.cloned.1.call-start = ((), (), s32[]{:S(2)}) async-start(), calls=%async_computation.5 | async-start | bytes 1310720 | tf_op jit(solution)/shard_map/while/body/eval_jaxpr/reduce_scatter | solution.py:168
  1443.0 59.4 %reduce-scatter.7.cloned.1.call-start = ((), (), s32[]{:S(2)}) async-start(), calls=%async_computation.6 | async-start | bytes 1310720 | tf_op jit(solution)/shard_map/while/body/eval_jaxpr/reduce_scatter | solution.py:169
  1476.2 53.8 %reduce-scatter.5.cloned.1.call-start = ((), (), s32[]{:S(2)}) async-start(), calls=%async_computation.5 | async-start | bytes 1310720 | tf_op jit(solution)/shard_map/while/body/eval_jaxpr/reduce_scatter | solution.py:168
  1534.3 60.0 %reduce-scatter.11.cloned.1.call-start = ((), (), s32[]{:S(2)}) async-start(), calls=%async_computation.8 | async-start | bytes 163840 | tf_op jit(solution)/shard_map/while/body/eval_jaxpr/reduce_scatter | solution.py:169
  1623.8 60.9 %reduce-scatter.11.cloned.1.call-start = ((), (), s32[]{:S(2)}) async-start(), calls=%async_computation.8 | async-start | bytes 163840 | tf_op jit(solution)/shard_map/while/body/eval_jaxpr/reduce_scatter | solution.py:169
  1663.1 49.1 %reduce-scatter.9.cloned.1.call-start = ((), (), s32[]{:S(2)}) async-start(), calls=%async_computation.7 | async-start | bytes 1310720 | tf_op jit(solution)/shard_map/while/body/eval_jaxpr/reduce_scatter | solution.py:168
  1714.1 60.9 %reduce-scatter.11.cloned.1.call-start = ((), (), s32[]{:S(2)}) async-start(), calls=%async_computation.8 | async-start | bytes 163840 | tf_op jit(solution)/shard_map/while/body/eval_jaxpr/reduce_scatter | solution.py:169
  1753.4 49.2 %reduce-scatter.9.cloned.1.call-start = ((), (), s32[]{:S(2)}) async-start(), calls=%async_computation.7 | async-start | bytes 1310720 | tf_op jit(solution)/shard_map/while/body/eval_jaxpr/reduce_scatter | solution.py:168
  1804.6 60.9 %reduce-scatter.11.cloned.1.call-start = ((), (), s32[]{:S(2)}) async-start(), calls=%async_computation.8 | async-start | bytes 163840 | tf_op jit(solution)/shard_map/while/body/eval_jaxpr/reduce_scatter | solution.py:169
  1843.9 49.0 %reduce-scatter.9.cloned.1.call-start = ((), (), s32[]{:S(2)}) async-start(), calls=%async_computation.7 | async-start | bytes 1310720 | tf_op jit(solution)/shard_map/while/body/eval_jaxpr/reduce_scatter | solution.py:168
  1895.0 60.9 %reduce-scatter.11.cloned.1.call-start = ((), (), s32[]{:S(2)}) async-start(), calls=%async_computation.8 | async-start | bytes 163840 | tf_op jit(solution)/shard_map/while/body/eval_jaxpr/reduce_scatter | solution.py:169
  1934.3 49.1 %reduce-scatter.9.cloned.1.call-start = ((), (), s32[]{:S(2)}) async-start(), calls=%async_computation.7 | async-start | bytes 1310720 | tf_op jit(solution)/shard_map/while/body/eval_jaxpr/reduce_scatter | solution.py:168
  1985.4 60.8 %reduce-scatter.11.cloned.1.call-start = ((), (), s32[]{:S(2)}) async-start(), calls=%async_computation.8 | async-start | bytes 163840 | tf_op jit(solution)/shard_map/while/body/eval_jaxpr/reduce_scatter | solution.py:169
  2024.7 49.2 %reduce-scatter.9.cloned.1.call-start = ((), (), s32[]{:S(2)}) async-start(), calls=%async_computation.7 | async-start | bytes 1310720 | tf_op jit(solution)/shard_map/while/body/eval_jaxpr/reduce_scatter | solution.py:168
  2075.8 60.9 %reduce-scatter.11.cloned.1.call-start = ((), (), s32[]{:S(2)}) async-start(), calls=%async_computation.8 | async-start | bytes 163840 | tf_op jit(solution)/shard_map/while/body/eval_jaxpr/reduce_scatter | solution.py:169
  2115.2 49.0 %reduce-scatter.9.cloned.1.call-start = ((), (), s32[]{:S(2)}) async-start(), calls=%async_computation.7 | async-start | bytes 1310720 | tf_op jit(solution)/shard_map/while/body/eval_jaxpr/reduce_scatter | solution.py:168
  2166.2 60.9 %reduce-scatter.11.cloned.1.call-start = ((), (), s32[]{:S(2)}) async-start(), calls=%async_computation.8 | async-start | bytes 163840 | tf_op jit(solution)/shard_map/while/body/eval_jaxpr/reduce_scatter | solution.py:169
  2205.5 49.2 %reduce-scatter.9.cloned.1.call-start = ((), (), s32[]{:S(2)}) async-start(), calls=%async_computation.7 | async-start | bytes 1310720 | tf_op jit(solution)/shard_map/while/body/eval_jaxpr/reduce_scatter | solution.py:168
  2256.7 108.4 %all-reduce.28.cloned.1.call-start = ((), (), s32[]{:S(2)}) async-start(), calls=%async_computation.4 | async-start | bytes 4128768 | tf_op jit(solution)/shard_map/psum | solution.py:254
  (563 other events, 5208.1 us)
Sparse Core Ops, SparseCore 0:
  848.8 25.7 reduce-scatter.6
  877.3 24.8 reduce-scatter.4
  938.3 26.0 reduce-scatter.6
  967.0 24.8 reduce-scatter.4
  1027.9 26.0 reduce-scatter.6
  1056.6 24.9 reduce-scatter.4
  1117.5 26.0 reduce-scatter.6
  1146.4 24.8 reduce-scatter.4
  1207.4 26.0 reduce-scatter.6
  1236.0 24.8 reduce-scatter.4
  1297.0 26.0 reduce-scatter.6
  1325.6 24.8 reduce-scatter.4
  1386.6 26.1 reduce-scatter.6
  1415.3 24.8 reduce-scatter.4
  1476.3 26.0 reduce-scatter.6
  1505.0 24.9 reduce-scatter.4
  1572.9 21.3 reduce-scatter.10
  1596.9 24.8 reduce-scatter.8
  1663.2 21.4 reduce-scatter.10
  1687.2 24.8 reduce-scatter.8
  1753.6 21.3 reduce-scatter.10
  1777.7 24.8 reduce-scatter.8
  1844.0 21.4 reduce-scatter.10
  1868.1 24.8 reduce-scatter.8
  1934.4 21.4 reduce-scatter.10
  1958.4 24.8 reduce-scatter.8
  2024.8 21.3 reduce-scatter.10
  2048.9 24.8 reduce-scatter.8
  2115.3 21.4 reduce-scatter.10
  2139.3 24.8 reduce-scatter.8
  2205.6 21.3 reduce-scatter.10
  2229.8 24.8 reduce-scatter.8
Sparse Core Ops, SparseCore 1:
  2262.2 102.8 all-reduce.27
where the time goes:
time: 2400 us; the launch traced here: 2380 us
  matrix products  789 us (33%)
  waiting for transfers between devices  614 us (26%)
  local copies, waits for them, and re-layouts  437 us (18%)
  starting transfers between devices  204 us (8%)
  other arithmetic  163 us (7%)
  blocking collectives  142 us (6%)
    dot_general x576, matrix products, apply_taps(): jnp.einsum('oc,ncyx->noyx', taps[3 * row_off + col_off], padded[:, :, fir...  608 us
    reduce_scatter x16, waiting for transfers between devices, retreat(): lax.psum_scatter(toward_hidden, 'gate', scatter_dimension=1, tiled=True)  419 us
    dot_general x288, matrix products, weight_terms(): jnp.einsum('noyx,ncyx->oc', rounded, shifted[:, :, row_off:row_off + own_...  181 us
    ppermute x34, starting transfers between devices, extended(): before = lax.ppermute(last, axis, up)  149 us
    all_gather x17, blocking collectives, spread(): gathered = lax.all_gather(hidden_now, 'gate', axis=1, tiled=True)  119 us
    reduce_scatter x16, waiting for transfers between devices, retreat(): lax.psum_scatter(toward_input, 'gate', scatter_dimension=1, tiled=True)  114 us
    psum x1, waiting for transfers between devices, per_device(): lax.psum((encoder_sums[2], encoder_sums[3], encoder_sums[4], encoder_sums...  76 us
    add x32, local copies, waits for them, and re-layouts, apply_taps(): total = moved if total is None else total + moved  68.7 us
  transfers between devices with their start and end apart: 101, of which 34 were waited for; matrix products, arithmetic and copies ran while one was open for 35% of the time, Pallas kernels for 0%

commit v1 on v0

v1 whole, which is shorter than its diff:
```python
import functools

import jax
import jax.numpy as jnp
from jax import lax
from jax.experimental import pallas as pl
from jax.experimental.pallas import tpu as pltpu
from jax.sharding import PartitionSpec as P

F32 = jnp.float32
BF16 = jnp.bfloat16


def ring(b):
    n = lax.axis_size("rows")
    k = (b - n // 4) % n
    return 2 * k if k < n // 2 else 2 * (n - 1 - k) + 1


def axis_sizes():
    return lax.axis_size("rows"), lax.axis_size("gate")


def block_perm(step):
    n = lax.axis_size("rows")
    return [(ring(b), ring((b + step) % n)) for b in range(n)]


def shuffle(value, d, home=False):
    n, m = axis_sizes()
    pairs = [(r * m + g, ring(r) * m + (g ^ d)) for r in range(n) for g in range(m)]
    if home:
        pairs = [(j, i) for i, j in pairs]
    return lax.ppermute(value, ("rows", "gate"), pairs)


def pick(value, index):
    return lax.dynamic_index_in_dim(value, index, 0, keepdims=False)


def to_images(value, g):
    m = lax.axis_size("gate")
    return [shuffle(pick(value, g ^ d), d) for d in range(m)]


def in_order(pieces, g):
    stacked = jnp.stack(pieces)
    return jnp.stack([pick(stacked, j ^ g) for j in range(len(pieces))])


def neighbours(first_row, last_row):
    above = lax.ppermute(last_row, "rows", block_perm(1))
    below = lax.ppermute(first_row, "rows", block_perm(-1))
    return above, below


def call(kernel, outs, ins, scratch=(), aliases=None, flops=0, name=None):
    size = sum(x.size * x.dtype.itemsize for x in ins)
    specs = [
        pl.BlockSpec(memory_space=pltpu.SMEM if x.dtype == jnp.int32 else pltpu.VMEM) for x in ins
    ]
    ins = [
        x if x.dtype == jnp.int32 else pltpu.with_memory_space_constraint(x, pltpu.VMEM)
        for x in ins
    ]
    return pl.pallas_call(
        kernel,
        out_shape=[pltpu.VMEM(shape, dtype) for shape, dtype in outs],
        in_specs=specs,
        out_specs=[pl.BlockSpec(memory_space=pltpu.VMEM) for _ in outs],
        scratch_shapes=list(scratch),
        input_output_aliases=aliases or {},
        cost_estimate=pl.CostEstimate(flops=flops, bytes_accessed=size, transcendentals=0),
        compiler_params=pltpu.CompilerParams(vmem_limit_bytes=16 * 1024 * 1024),
        name=name,
    )(*ins)


def sigmoid(v):
    return 0.5 * jnp.tanh(0.5 * v) + 0.5


def column_shift(value, delta):
    if delta == 0:
        return value
    lane = lax.broadcasted_iota(jnp.int32, (value.shape[0], 128), 1)
    parts = []
    for k in range(value.shape[1] // 128):
        moved = pltpu.roll(value[:, k * 128 : (k + 1) * 128], (-delta) % 128, 1)
        parts.append(jnp.where(lane == (127 if delta > 0 else 0), 0.0, moved))
    return jnp.concatenate(parts, axis=1)


def spread_taps(g, taps, base, channels, rows, ordered):
    groups = 1 if ordered else 4
    part = channels // groups
    width = rows[0].shape[1]
    for r, row in enumerate(rows):
        for d in range(groups):
            start = 0 if ordered else pl.multiple_of((d ^ g) * part, part)
            value = row[pl.ds(d * part, part), :].astype(F32)
            for e in range(3):
                moved = column_shift(value, e - 1).astype(BF16)
                for a in range(3):
                    y = r - a
                    if 0 <= y < 2:
                        at = base + (3 * a + e) * channels + start
                        taps[pl.ds(at, part), y * width : (y + 1) * width] = moved


def clear_ends(place, taps, base, channels, width):
    @pl.when(place[1] == 0)
    def _():
        taps[base : base + channels, :width] = jnp.zeros((channels, width), BF16)

    @pl.when(place[2] == 0)
    def _():
        taps[base + 2 * channels : base + 3 * channels, width:] = jnp.zeros(
            (channels, width), BF16
        )


def gates_forward(z, memory, bias, peep, out0, out1, new_memory, acts):
    width = out0.shape[1]
    for d in range(4):
        rows = slice(d * 32, d * 32 + 32)
        b = [bias[d * 128 + q * 32 : d * 128 + q * 32 + 32, :] for q in range(4)]
        p = [peep[q * 128 + d * 32 : q * 128 + d * 32 + 32, :] for q in range(3)]
        for k in range(2 * width // 128):
            cols = slice(k * 128, k * 128 + 128)
            a = [z[d * 128 + q * 32 : d * 128 + q * 32 + 32, cols] + b[q] for q in range(4)]
            c = memory[rows, cols]
            i = sigmoid(a[0] + p[0] * c)
            f = sigmoid(a[1] + p[1] * c)
            gg = jnp.tanh(a[3])
            cn = f * c + i * gg
            o = sigmoid(a[2] + p[2] * cn)
            h = (o * jnp.tanh(cn)).astype(BF16)
            acts[0, rows, cols] = i
            acts[1, rows, cols] = f
            acts[2, rows, cols] = o
            acts[3, rows, cols] = gg
            new_memory[rows, cols] = cn
            if k * 128 < width:
                out0[rows, cols] = h
            else:
                out1[rows, k * 128 - width : k * 128 - width + 128] = h


def encoder_kernel(
    g, weights, h0, h1, up, down, frame, memory, bias, peep, out0, out1, new_memory, acts, taps, z
):
    width = h0.shape[1]
    spread_taps(g[0], taps, 0, 128, (up, h0, h1, down), False)
    clear_ends(g, taps, 0, 384, width)
    spread_taps(
        g[0], taps, 1152, 16, [frame.at[:, r * width : (r + 1) * width] for r in range(4)], True
    )
    taps[1296:, :] = jnp.zeros((taps.shape[0] - 1296, taps.shape[1]), BF16)
    z[...] = jnp.dot(weights[...], taps[...], preferred_element_type=F32)
    gates_forward(z, memory, bias, peep, out0, out1, new_memory, acts)


def forecaster_kernel(
    g, weights, e0, e1, eup, edown, h0, h1, up, down, memory, bias, peep,
    out0, out1, new_memory, acts, taps, z,
):
    spread_taps(g[0], taps, 0, 128, (eup, e0, e1, edown), False)
    spread_taps(g[0], taps, 1152, 128, (up, h0, h1, down), False)
    clear_ends(g, taps, 0, 384, h0.shape[1])
    clear_ends(g, taps, 1152, 384, h0.shape[1])
    z[...] = jnp.dot(weights[...], taps[...], preferred_element_type=F32)
    gates_forward(z, memory, bias, peep, out0, out1, new_memory, acts)


def backward_kernel(first, encoder, *refs):
    it = iter(refs)
    place = next(it)
    g = place[0]
    inside = [place[1].astype(F32), place[2].astype(F32)]
    weights, acts, memory, before, peep = (next(it) for _ in range(5))
    if encoder:
        outside = [next(it) for _ in range(3)]
    else:
        outside = [next(it) for _ in range(4)]
    sums_in = None
    if not first:
        sums_in, dc_in, inner_in, above_in, below_in = (next(it) for _ in range(5))
    dz3, dc_out, sums = (next(it) for _ in range(3))
    r_inner, r_up, r_down, k_inner, k_up, k_down = (next(it) for _ in range(6))
    d_ref = next(it)
    width = r_up.shape[1]
    lanes = 2 * width
    own = k_up.shape[0]

    for d in range(4):
        rows = slice(d * 32, d * 32 + 32)
        natural = pl.ds(pl.multiple_of((d ^ g) * 32, 32), 32)
        p = [peep[q * 128 + d * 32 : q * 128 + d * 32 + 32, :] for q in range(3)]
        totals = [jnp.zeros((32, 128), F32) for _ in range(7)]
        for k in range(lanes // 128):
            cols = slice(k * 128, k * 128 + 128)
            y = k * 128 // width
            part = slice(k * 128 - y * width, k * 128 - y * width + 128)
            i, f, o, gg = (acts[q, rows, cols] for q in range(4))
            c, c_old = memory[rows, cols], before[rows, cols]
            if encoder:
                inner, above, below = outside
                dh = inner[natural, cols] + inside[y] * (above, below)[y][natural, part].astype(F32)
            else:
                dh = outside[d][y, :, part].astype(F32)
            if not first:
                halo = (above_in, below_in)[y][natural, part].astype(F32)
                dh += inner_in[natural, cols] + inside[y] * halo
            t = jnp.tanh(c)
            do = dh * t * o * (1.0 - o)
            dc = dh * o * (1.0 - t * t) + do * p[2]
            if not first:
                dc += dc_in[rows, cols]
            di = dc * gg * i * (1.0 - i)
            df = dc * c_old * f * (1.0 - f)
            dg = dc * i * (1.0 - gg * gg)
            dc_out[rows, cols] = dc * f + di * p[0] + df * p[1]
            for q, v in enumerate((di, df, do, dg)):
                totals[q] += v
                at = d * 128 + q * 32
                for e in range(3):
                    dz3[e * 512 + at : e * 512 + at + 32, cols] = column_shift(v, 1 - e).astype(
                        BF16
                    )
            for q, v in enumerate((di * c_old, df * c_old, do * c)):
                totals[4 + q] += v
        for q in range(7):
            at = slice(q * 128 + d * 32, q * 128 + d * 32 + 32)
            sums[at, :] = totals[q] if first else totals[q] + sums_in[at, :]

    d_ref[...] = jnp.dot(weights[...], dz3[...], preferred_element_type=F32)
    first_row, last_row = slice(0, width), slice(width, lanes)
    for base, size, inner, up, down in ((0, 128, r_inner, r_up, r_down), (384, own, k_inner, k_up, k_down)):
        a0, a1, a2 = (slice(base + a * size, base + (a + 1) * size) for a in range(3))
        inner[:, first_row] = d_ref[a1, first_row] + d_ref[a0, last_row]
        inner[:, last_row] = d_ref[a1, last_row] + d_ref[a2, first_row]
        up[...] = d_ref[a0, first_row].astype(BF16)
        down[...] = d_ref[a2, last_row].astype(BF16)


def ordered(rows):
    first, last, above, below = rows
    return [above, first, last, below]


def weight_kernel(first, encoder, *refs):
    it = iter(refs)
    place = next(it)
    g = place[0]
    dz3 = next(it)
    h_rows = ordered([next(it) for _ in range(4)])
    other = next(it) if encoder else ordered([next(it) for _ in range(4)])
    acc_in = None if first else next(it)
    acc, seen = next(it), next(it)
    width = h_rows[0].shape[1]

    def lay(rows, base, stride):
        for r, row in enumerate(rows):
            for a in range(3):
                y = r - a
                if 0 <= y < 2:
                    for d in range(4):
                        at = pl.multiple_of(base + a * stride + (d ^ g) * 32, 32)
                        seen[pl.ds(at, 32), y * width : (y + 1) * width] = row[
                            d * 32 : d * 32 + 32, :
                        ]

    if encoder:
        lay(h_rows, 0, 128)
        clear_ends(place, seen, 0, 128, width)
        for a in range(3):
            seen[384 + 16 * a : 400 + 16 * a, :] = other[:, a * width : (a + 2) * width]
        seen[432:, :] = jnp.zeros((seen.shape[0] - 432, seen.shape[1]), BF16)
    else:
        lay(other, 0, 256)
        lay(h_rows, 128, 256)
        clear_ends(place, seen, 0, 256, width)
    for n in range(acc.shape[1] // 256):
        cols = slice(n * 256, n * 256 + 256)
        term = lax.dot_general(
            dz3[...], seen[cols, :], (((1,), (1,)), ((), ())), preferred_element_type=F32
        )
        acc[:, cols] = term if first else acc_in[:, cols] + term


def encoder_step(g, weights, state, frame, bias, peep):
    h0, h1, up, down, memory = state
    lanes = memory.shape[1]
    return call(
        encoder_kernel,
        [(h0.shape, BF16), (h0.shape, BF16), (memory.shape, F32), ((4,) + memory.shape, F32)],
        [g, weights, h0, h1, up, down, frame, memory, bias, peep],
        [pltpu.VMEM((weights.shape[1], lanes), BF16), pltpu.VMEM((512, lanes), F32)],
        flops=2 * 512 * weights.shape[1] * lanes,
        name="encoder_step",
    )


def forecaster_step(g, weights, encoded, state, bias, peep):
    h0, h1, up, down, memory = state
    lanes = memory.shape[1]
    return call(
        forecaster_kernel,
        [(h0.shape, BF16), (h0.shape, BF16), (memory.shape, F32), ((4,) + memory.shape, F32)],
        [g, weights, *encoded, h0, h1, up, down, memory, bias, peep],
        [pltpu.VMEM((weights.shape[1], lanes), BF16), pltpu.VMEM((512, lanes), F32)],
        flops=2 * 512 * weights.shape[1] * lanes,
        name="forecaster_step",
    )


def backward_step(g, weights, acts, memory, before, peep, outside, carried, encoder):
    lanes = memory.shape[1]
    own = 16 if encoder else 128
    row = lanes // 2
    return call(
        functools.partial(backward_kernel, carried is None, encoder),
        [
            ((1536, lanes), BF16), ((128, lanes), F32), ((896, 128), F32),
            ((128, lanes), F32), ((128, row), BF16), ((128, row), BF16),
            ((own, lanes), F32), ((own, row), BF16), ((own, row), BF16),
        ],
        [g, weights, acts, memory, before, peep, *outside, *(carried or ())],
        [pltpu.VMEM((weights.shape[0], lanes), F32)],
        flops=2 * weights.shape[0] * weights.shape[1] * lanes,
        name="encoder_back" if encoder else "forecaster_back",
    )


def weight_step(g, dz3, h_rows, other, acc, encoder):
    lanes = dz3.shape[1]
    columns = 512 if encoder else 768
    ins = [g, dz3, *h_rows, *([other] if encoder else other)]
    return call(
        functools.partial(weight_kernel, acc is None, encoder),
        [((1536, columns), F32)],
        ins + ([] if acc is None else [acc]),
        [pltpu.VMEM((columns, lanes), BF16)],
        aliases=None if acc is None else {len(ins): 0},
        flops=2 * 1536 * columns * lanes,
        name="encoder_weights" if encoder else "forecaster_weights",
    )[0]


def gather_gate(value):
    across = lax.ppermute(value, "gate", swap_perm(2))
    beside = lax.ppermute(jnp.stack([value, across]), "gate", swap_perm(1))
    return jnp.stack([value, beside[0], across, beside[1]])


def swap_perm(d):
    return [(i, i ^ d) for i in range(lax.axis_size("gate"))]


def reduce_gate(parts, wire):
    beside = lax.ppermute(jnp.stack([parts[1], parts[3]]).astype(wire), "gate", swap_perm(1))
    far = parts[2] + beside[1].astype(F32)
    near = parts[0] + beside[0].astype(F32)
    return near + lax.ppermute(far.astype(wire), "gate", swap_perm(2)).astype(F32)


def reduce_rows(value, wire):
    n = lax.axis_size("rows")
    r = lax.axis_index("rows")
    bits = [1 << b for b in range(n.bit_length() - 1)]
    for bit in bits:
        halves = value.reshape((2, value.shape[0] // 2) + value.shape[1:])
        mine = (r // bit) % 2
        given = pick(halves, 1 - mine).astype(wire)
        got = lax.ppermute(given, "rows", [(i, i ^ bit) for i in range(n)])
        value = pick(halves, mine) + got.astype(F32)
    value = value.astype(wire)
    for bit in reversed(bits):
        mine = (r // bit) % 2
        got = lax.ppermute(value, "rows", [(i, i ^ bit) for i in range(n)])
        value = jnp.concatenate([jnp.where(mine == 0, value, got), jnp.where(mine == 0, got, value)])
    return value.astype(F32)


def sum_rows(value):
    n = lax.axis_size("rows")
    for b in range(n.bit_length() - 1):
        value = value + lax.ppermute(value, "rows", [(i, i ^ (1 << b)) for i in range(n)])
    return value


def per_device(
    frames,
    validity,
    encoding_start_hidden,
    encoding_start_cell,
    encoding_input_kernel,
    encoding_recurrent_kernel,
    encoding_gate_bias,
    encoding_peephole_weight,
    predicting_start_hidden,
    predicting_start_cell,
    predicting_input_kernel,
    predicting_recurrent_kernel,
    predicting_gate_bias,
    predicting_peephole_weight,
    cotangent,
):
    n, m = axis_sizes()
    gi = lax.axis_index("gate")
    r = lax.axis_index("rows")
    block = sum(jnp.where(r == ring(b), b, 0) for b in range(n))
    inside = (block > 0, block < n - 1)
    g = jnp.stack([gi, *inside]).astype(jnp.int32)
    steps, images, channels, rows, across = frames.shape
    own = images // m
    width = own * across
    lanes = rows * width
    local = encoding_start_cell.shape[1]

    def state_pieces(value):
        value = value.reshape(m, own, local, rows, across).transpose(0, 3, 2, 1, 4)
        return to_images(value.reshape(m, rows, local, width), gi)

    def start(hidden, cell):
        h = jnp.concatenate(state_pieces(hidden), axis=1)
        c = state_pieces(cell)
        c = jnp.concatenate([jnp.concatenate([p[0], p[1]], axis=1) for p in c], axis=0)
        above, below = neighbours(h[0], h[1])
        return (h[0], h[1], above, below, c)

    valid = validity.astype(BF16)
    masked = frames * valid[None, :, None, :, :]

    mine = pick(masked.reshape(steps, m, own, channels, rows, across).swapaxes(0, 1), gi)
    mine = mine.transpose(0, 2, 3, 1, 4).reshape(steps, channels, rows, width)
    body = lax.ppermute(mine, "rows", [(b, ring(b)) for b in range(n)])
    above = lax.ppermute(mine[:, :, 1], "rows", [(b, ring((b + 1) % n)) for b in range(n)])
    below = lax.ppermute(mine[:, :, 0], "rows", [(b, ring((b - 1) % n)) for b in range(n)])
    above = jnp.where(inside[0], above, 0)
    below = jnp.where(inside[1], below, 0)
    padded = jnp.concatenate([above, body[:, :, 0], body[:, :, 1], below], axis=2)

    def flat(kernel):
        return kernel.reshape(kernel.shape[0] * kernel.shape[1], 9 * kernel.shape[3])

    def small(bias, peep):
        both = gather_gate(jnp.concatenate([bias, peep], axis=0))
        b = jnp.broadcast_to(both[:, :4].reshape(512, 1), (512, 128))
        p = jnp.broadcast_to(both[:, 4:].swapaxes(0, 1).reshape(384, 1), (384, 128))
        return b, p

    def turned(kernel):
        c = kernel.shape[1] // 9
        return kernel.reshape(512, 3, 3, c).transpose(1, 3, 2, 0).reshape(3 * c, 1536)

    enc_r = gather_gate(flat(encoding_recurrent_kernel)).reshape(512, 1152)
    enc_k = gather_gate(flat(encoding_input_kernel)).reshape(512, 144)
    enc_w = jnp.concatenate([enc_r, enc_k, jnp.zeros((512, 112), BF16)], axis=1)
    enc_bias, enc_peep = small(encoding_gate_bias, encoding_peephole_weight)
    fc_k = gather_gate(flat(predicting_input_kernel)).reshape(512, 1152)
    fc_r = gather_gate(flat(predicting_recurrent_kernel)).reshape(512, 1152)
    fc_w = jnp.concatenate([fc_k, fc_r], axis=1)
    fc_bias, fc_peep = small(predicting_gate_bias, predicting_peephole_weight)

    enc_state = start(encoding_start_hidden, encoding_start_cell)
    fc_state = start(predicting_start_hidden, predicting_start_cell)

    enc_back = jnp.concatenate([turned(enc_r), turned(enc_k)], axis=0)
    fc_back = jnp.concatenate([turned(fc_r), turned(fc_k)], axis=0)

    incoming = cotangent * valid[None, :, None, :, :]
    incoming = incoming.reshape(steps, m, own, local, rows, across).transpose(1, 0, 4, 3, 2, 5)
    incoming = to_images(incoming.reshape(m, steps, rows, local, width), gi)

    enc_states, fc_states, enc_acts, fc_acts = [enc_state], [fc_state], [], []
    for t in range(steps + 1):
        if t < steps:
            h0, h1, memory, acts = encoder_step(
                g, enc_w, enc_states[-1], padded[t], enc_bias, enc_peep
            )
            enc_acts.append(acts)
            enc_states.append((h0, h1, *neighbours(h0, h1), memory))
        if t > 0:
            h0, h1, memory, acts = forecaster_step(
                g, fc_w, enc_states[t][:4], fc_states[-1], fc_bias, fc_peep
            )
            fc_acts.append(acts)
            more = neighbours(h0, h1) if t < steps else (None, None)
            fc_states.append((h0, h1, *more, memory))

    sent = [jnp.stack([s[0], s[1]]).reshape(rows, m, local, width) for s in fc_states[1:]]
    sent = jnp.stack(sent)
    pieces = [shuffle(sent[:, :, d], d, True) for d in range(m)]
    predicted = in_order(pieces, gi).reshape(m, steps, rows, local, own, across)
    predicted = predicted.transpose(1, 0, 4, 3, 2, 5).reshape(steps, images, local, rows, across)

    def after(step):
        dz3, dc, sums, r_inner, r_up, r_down, k_inner, k_up, k_down = step
        r_above, r_below = neighbours(r_up, r_down)
        k_above, k_below = neighbours(k_up, k_down)
        return (sums, dc, r_inner, r_above, r_below), (k_inner, k_above, k_below)

    fc_carry = enc_carry = fc_acc = enc_acc = None
    into = [None] * steps
    toward_frames = [None] * steps
    for t in range(steps - 1, -2, -1):
        if t >= 0:
            step = backward_step(
                g, fc_back, fc_acts[t], fc_states[t + 1][4], fc_states[t][4], fc_peep,
                [p[t] for p in incoming], fc_carry, False,
            )
            fc_carry, into[t] = after(step)
            fc_acc = weight_step(
                g, step[0], fc_states[t][:4], enc_states[t + 1][:4], fc_acc, False
            )
        if t + 1 < steps:
            t += 1
            step = backward_step(
                g, enc_back, enc_acts[t], enc_states[t + 1][4], enc_states[t][4], enc_peep,
                into[t], enc_carry, True,
            )
            enc_carry, toward_frames[t] = after(step)
            enc_acc = weight_step(g, step[0], enc_states[t][:4], padded[t], enc_acc, True)

    def beside(above, below):
        return jnp.concatenate(
            [jnp.where(inside[0], above, 0), jnp.where(inside[1], below, 0)], axis=1
        )

    def state_gradient(pieces):
        pieces = [shuffle(p, d, True) for d, p in enumerate(pieces)]
        value = in_order(pieces, gi).reshape(m, local, rows, own, across)
        return value.transpose(0, 3, 1, 2, 4).reshape(images, local, rows, across)

    def finish_state(carry):
        sums, dc, inner, above, below = carry
        dh = inner + beside(above, below).astype(F32)
        dh = dh.reshape(m, local, lanes)
        dc = dc.reshape(m, local, lanes)
        return (
            state_gradient([pick(dh, gi ^ d) for d in range(m)]),
            state_gradient([dc[d] for d in range(m)]),
        )

    inner = jnp.stack([x[0] for x in toward_frames])
    halo = jnp.stack([beside(x[1], x[2]) for x in toward_frames])
    dframes = (inner + halo.astype(F32)).reshape(steps, m, channels // m, rows, own, across)
    dframes = dframes.swapaxes(0, 1)
    pieces = [shuffle(pick(dframes, gi ^ d), d, True) for d in range(m)]
    frames_gradient = in_order(pieces, gi).transpose(1, 0, 4, 2, 3, 5)
    frames_gradient = frames_gradient.reshape(steps, images, channels // m, rows, across)
    frames_gradient = frames_gradient * validity.astype(F32)[None, :, None, :, :]

    def total(acc):
        acc = acc.reshape(3, m, 4 * local, acc.shape[1])
        got = reduce_gate([acc[:, d] for d in range(m)], BF16)
        return reduce_rows(got.reshape(3 * 4 * local, -1), BF16).reshape(3, 4, local, -1)

    def small_total(carries):
        both = jnp.stack([c[0].sum(axis=1).reshape(7, m, local) for c in carries])
        return sum_rows(reduce_gate([both[:, :, d] for d in range(m)], F32))

    fc_total = total(fc_acc).reshape(3, 4, local, 3, 2, 128)
    fc_total = fc_total.transpose(4, 1, 2, 3, 0, 5).reshape(2, 4, local, 9, 128)
    enc_total = total(enc_acc)
    enc_r_grad = enc_total[..., :384].reshape(3, 4, local, 3, 128)
    enc_r_grad = enc_r_grad.transpose(1, 2, 3, 0, 4).reshape(4, local, 9, 128)
    enc_k_grad = enc_total[..., 384:432].reshape(3, 4, local, 3, 16)
    enc_k_grad = enc_k_grad.transpose(1, 2, 3, 0, 4).reshape(4, local, 9, 16)
    smalls = small_total((enc_carry, fc_carry))
    enc_hidden, enc_cell = finish_state(enc_carry)
    fc_hidden, fc_cell = finish_state(fc_carry)
    return (
        predicted,
        frames_gradient,
        enc_hidden,
        enc_cell,
        enc_k_grad,
        enc_r_grad,
        smalls[0, :4],
        smalls[0, 4:],
        fc_hidden,
        fc_cell,
        fc_total[0],
        fc_total[1],
        smalls[1, :4],
        smalls[1, 4:],
    )


def solution(mesh):
    state = P(None, "gate", "rows", None)
    kernel = P(None, "gate", None, None)
    small = P(None, "gate")
    layer = (state, state, kernel, kernel, small, small)
    return jax.shard_map(
        per_device,
        mesh=mesh,
        in_specs=(
            P(None, None, None, "rows", None),
            P(None, "rows", None),
            *layer,
            *layer,
            P(None, None, "gate", "rows", None),
        ),
        out_specs=(
            P(None, None, "gate", "rows", None),
            P(None, None, "gate", "rows", None),
            *layer,
            *layer,
        ),
        check_vma=False,
    )
```

time: 2400 us -> 793 us (0.33)
  matrix products: 789 us -> 0 us
  waiting for transfers between devices: 614 us -> 135 us
  local copies, waits for them, and re-layouts: 437 us -> 240 us
  blocking collectives: 142 us -> 0 us
  other arithmetic: 163 us -> 42 us
  Pallas kernels: 0 us -> 115 us
  starting transfers between devices: 204 us -> 239 us
    dot_general x864 -> x0, matrix products: 789 us -> none  [the longest x576 608 us: apply_taps(): jnp.einsum('oc,ncyx->noyx', taps[3 * row_off + col_off], padded[:, :, fir...]
    reduce_scatter x32 -> x0, waiting for transfers between devices: 533 us -> none  [the longest x16 419 us: retreat(): lax.psum_scatter(toward_hidden, 'gate', scatter_dimension=1, tiled=True)]
    unnamed x71 -> x920, local copies, waits for them, and re-layouts: 9.56 us -> 154 us
    ppermute x68 -> x178, waiting for transfers between devices: 5.03 us -> 135 us  [the longest x44 58.5 us: shuffle(): return lax.ppermute(value, ('rows', 'gate'), pairs)]
    all_gather x17 -> x0, blocking collectives: 119 us -> none  [spread(): gathered = lax.all_gather(hidden_now, 'gate', axis=1, tiled=True)]
    pallas_call x0 -> x48, Pallas kernels: none -> 115 us  [call(): pl.pallas_call(kernel, out_shape=[pltpu.VMEM(shape, dtype) for shape, dty...]
    add x48 -> x0, local copies, waits for them, and re-layouts: 78.7 us -> none  [the longest x32 68.7 us: apply_taps(): total = moved if total is None else total + moved]
    psum x1 -> x0, waiting for transfers between devices: 76 us -> none  [per_device(): lax.psum((encoder_sums[2], encoder_sums[3], encoder_sums[4], encoder_sums...]
  transfers between devices with their start and end apart: 101 -> 178, of which waited for: 34 -> 57; matrix products, arithmetic and copies ran while one was open for 35% -> 17% of each run, Pallas kernels for 0% -> 14%
where the time goes in v1:
time: 793 us; the launch traced here: 778 us
  local copies, waits for them, and re-layouts  240 us (30%)
  starting transfers between devices  239 us (30%)
  waiting for transfers between devices  135 us (17%)
  Pallas kernels  115 us (15%)
  other arithmetic  42 us (5%)
    unnamed x920, local copies, waits for them, and re-layouts  154 us
    pallas_call x48, Pallas kernels, call(): pl.pallas_call(kernel, out_shape=[pltpu.VMEM(shape, dtype) for shape, dty...  115 us
    ppermute x44, starting transfers between devices, shuffle(): return lax.ppermute(value, ('rows', 'gate'), pairs)  89.5 us
    ppermute x44, waiting for transfers between devices, shuffle(): return lax.ppermute(value, ('rows', 'gate'), pairs)  58.5 us
    ppermute x49, starting transfers between devices, neighbours(): above = lax.ppermute(last_row, 'rows', block_perm(1))  53.9 us
    ppermute x49, starting transfers between devices, neighbours(): below = lax.ppermute(first_row, 'rows', block_perm(-1))  48.8 us
    ppermute x49, waiting for transfers between devices, neighbours(): above = lax.ppermute(last_row, 'rows', block_perm(1))  23.7 us
    ppermute x6, waiting for transfers between devices, reduce_rows(): got = lax.ppermute(given, 'rows', [(i, i ^ bit) for i in range(n)])  16.9 us
  transfers between devices with their start and end apart: 178, of which 57 were waited for; matrix products, arithmetic and copies ran while one was open for 17% of the time, Pallas kernels for 14%

profile of v1, /device:TPU:0, one launch (start us, length us, event | category | flops | bytes accessed | tf_op | source)
XLA Modules:
  0.0 777.6 jit_solution(3443694509300809188)
XLA Ops:
  11.6 4.4 collective-permute-start.15
  40.2 3.5 collective-permute-done.9
  52.8 6.0 collective-permute-start.25
  64.0 5.0 collective-permute-start.27
  70.6 4.2 collective-permute-done.28
  79.2 5.4 collective-permute-start.16
  89.1 4.0 collective-permute-done.14
  93.2 4.6 collective-permute-done.20
  97.8 4.8 collective-permute-start.19
  104.4 3.8 collective-permute-done.18
  108.3 5.8 collective-permute-start.17
  116.0 4.8 collective-permute-done.34
  120.8 4.9 collective-permute-start.33
  127.6 3.8 collective-permute-done.32
  131.5 5.8 collective-permute-start.31
  140.8 5.0 collective-permute-start.69
  148.7 4.1 collective-permute-done.69
  152.8 4.2 collective-permute-start.71
  158.4 4.0 collective-permute-start.72
  339.8 3.6 forecaster_back.10
  419.8 3.4 copy.334
  435.3 3.6 forecaster_back.12
  480.6 3.5 forecaster_back.13
  523.6 3.6 forecaster_back.14
  565.8 3.5 forecaster_back.15
  599.2 3.4 collective-permute-done.119
  660.6 3.7 collective-permute-start.143
  714.1 5.3 collective-permute-done.148
  722.8 4.8 collective-permute-done.149
  736.5 5.7 collective-permute-done.172
  750.7 3.7 collective-permute-done.174
  766.8 3.4 collective-permute-done.154
  (1549 shorter events, 631.8 us)
Async XLA Ops:
  2.6 167.7 %collective-permute-start.2 = (bf16[128,1152]{1,0:T(8,128)(2,1)}, bf16[128,1152]{1,0:T(8,128)(2,1)}, u32[]{:S(2)}, u32[]{:S(2)}) collective-permute-start(bf16[128,1152]{1,0:T(8,128)(2,1)} %bitcast.478), channel_id=1, source_target_pairs={{0,2},{1,3},{2,0},{3,1},{4,6},{5,7},{6,4},{7,5},{8,10},{9,11},{10,... | collective-permute-start | bytes 884744 | tf_op jit(solution)/shard_map/ppermute | solution.py:352
  6.6 166.9 %collective-permute-start = (bf16[128,1152]{1,0:T(8,128)(2,1)}, bf16[128,1152]{1,0:T(8,128)(2,1)}, u32[]{:S(2)}, u32[]{:S(2)}) collective-permute-start(bf16[128,1152]{1,0:T(8,128)(2,1)} %bitcast.479), channel_id=1, source_target_pairs={{0,2},{1,3},{2,0},{3,1},{4,6},{5,7},{6,4},{7,5},{8,10},{9,11},{10,... | collective-permute-start | bytes 884744 | tf_op jit(solution)/shard_map/ppermute | solution.py:352
  7.6 159.0 %collective-permute-start.4 = (bf16[128,1152]{1,0:T(8,128)(2,1)}, bf16[128,1152]{1,0:T(8,128)(2,1)}, u32[]{:S(2)}, u32[]{:S(2)}) collective-permute-start(bf16[128,1152]{1,0:T(8,128)(2,1)} %bitcast.477), channel_id=1, source_target_pairs={{0,2},{1,3},{2,0},{3,1},{4,6},{5,7},{6,4},{7,5},{8,10},{9,11},{10,... | collective-permute-start | bytes 884744 | tf_op jit(solution)/shard_map/ppermute | solution.py:352
  11.6 135.4 %collective-permute-start.15 = (bf16[8,16,2,256]{3,1,0,2:T(8,128)(2,1)}, bf16[8,16,2,256]{3,1,0,2:T(8,128)(2,1)}, u32[]{:S(2)}, u32[]{:S(2)}) collective-permute-start(bf16[8,16,2,256]{3,1,0,2:T(8,128)(2,1)} %reshape.309), channel_id=1, source_target_pairs={{0,12},{4,4},{8,0},{12,8},{16,16},{20,24},{24,28},{28,20},{1,13},{... | collective-permute-start | bytes 393224 | tf_op jit(solution)/shard_map/ppermute | solution.py:438
  170.3 56.9 %collective-permute-start.29 = (bf16[128,256]{1,0:T(8,128)(2,1)}, bf16[128,256]{1,0:T(8,128)(2,1)}, u32[]{:S(2)}, u32[]{:S(2)}) collective-permute-start(bf16[128,256]{1,0:T(8,128)(2,1)} %get-tuple-element.608.h1.refs_3_), channel_id=1, source_target_pairs={{12,4},{4,0},{0,8},{8,16},{16,24},{24,28},{28,20},{20,12},{13,5},{... | collective-permute-start | bytes 196616 | tf_op jit(solution)/shard_map/ppermute | solution.py:52
  173.4 53.7 %collective-permute-start.30 = (bf16[128,256]{1,0:T(8,128)(2,1)}, bf16[128,256]{1,0:T(8,128)(2,1)}, u32[]{:S(2)}, u32[]{:S(2)}) collective-permute-start(bf16[128,256]{1,0:T(8,128)(2,1)} %get-tuple-element.609.h0.refs_2_), channel_id=1, source_target_pairs={{12,20},{4,12},{0,4},{8,0},{16,8},{24,16},{28,24},{20,28},{13,21},... | collective-permute-start | bytes 196616 | tf_op jit(solution)/shard_map/ppermute | solution.py:53
  186.7 36.2 %collective-permute-start.23 = (bf16[128,256]{1,0:T(8,128)(2,1)S(1)}, bf16[128,256]{1,0:T(8,128)(2,1)S(1)}, u32[]{:S(2)}, u32[]{:S(2)}) collective-permute-start(bf16[128,256]{1,0:T(8,128)(2,1)S(1)} %get-tuple-element.223.e1.h1.refs_3_.refs_7_), channel_id=1, source_target_pairs={{12,4},{4,0},{0,8},{8,16},{16,24},{24,28},{28,20},{20,12},{13,5},{... | collective-permute-start | bytes 196616 | tf_op jit(solution)/shard_map/ppermute | solution.py:52
  188.0 34.9 %collective-permute-start.24 = (bf16[128,256]{1,0:T(8,128)(2,1)S(1)}, bf16[128,256]{1,0:T(8,128)(2,1)S(1)}, u32[]{:S(2)}, u32[]{:S(2)}) collective-permute-start(bf16[128,256]{1,0:T(8,128)(2,1)S(1)} %get-tuple-element.222.e0.h0.refs_2_.refs_6_), channel_id=1, source_target_pairs={{12,20},{4,12},{0,4},{8,0},{16,8},{24,16},{28,24},{20,28},{13,21},... | collective-permute-start | bytes 196616 | tf_op jit(solution)/shard_map/ppermute | solution.py:53
  311.7 36.4 %collective-permute-start.99 = (bf16[128,256]{1,0:T(8,128)(2,1)}, bf16[128,256]{1,0:T(8,128)(2,1)}, u32[]{:S(2)}, u32[]{:S(2)}) collective-permute-start(bf16[128,256]{1,0:T(8,128)(2,1)} %get-tuple-element.338), channel_id=1, source_target_pairs={{12,4},{4,0},{0,8},{8,16},{16,24},{24,28},{28,20},{20,12},{13,5},{... | collective-permute-start | bytes 196616 | tf_op jit(solution)/shard_map/ppermute | solution.py:52
  313.0 35.3 %collective-permute-start.100 = (bf16[128,256]{1,0:T(8,128)(2,1)}, bf16[128,256]{1,0:T(8,128)(2,1)}, u32[]{:S(2)}, u32[]{:S(2)}) collective-permute-start(bf16[128,256]{1,0:T(8,128)(2,1)} %get-tuple-element.339), channel_id=1, source_target_pairs={{12,20},{4,12},{0,4},{8,0},{16,8},{24,16},{28,24},{20,28},{13,21},... | collective-permute-start | bytes 196616 | tf_op jit(solution)/shard_map/ppermute | solution.py:53
  346.2 44.3 %collective-permute-start.77 = (bf16[128,256]{1,0:T(8,128)(2,1)}, bf16[128,256]{1,0:T(8,128)(2,1)}, u32[]{:S(2)}, u32[]{:S(2)}) collective-permute-start(bf16[128,256]{1,0:T(8,128)(2,1)} %get-tuple-element.291), channel_id=1, source_target_pairs={{12,4},{4,0},{0,8},{8,16},{16,24},{24,28},{28,20},{20,12},{13,5},{... | collective-permute-start | bytes 196616 | tf_op jit(solution)/shard_map/ppermute | solution.py:52
  348.1 45.0 %collective-permute-start.78 = (bf16[128,256]{1,0:T(8,128)(2,1)}, bf16[128,256]{1,0:T(8,128)(2,1)}, u32[]{:S(2)}, u32[]{:S(2)}) collective-permute-start(bf16[128,256]{1,0:T(8,128)(2,1)} %get-tuple-element.292), channel_id=1, source_target_pairs={{12,20},{4,12},{0,4},{8,0},{16,8},{24,16},{28,24},{20,28},{13,21},... | collective-permute-start | bytes 196616 | tf_op jit(solution)/shard_map/ppermute | solution.py:53
  375.5 35.6 %collective-permute-start.68 = (bf16[8,2,32,256]{3,2,1,0:T(8,128)(2,1)}, bf16[8,2,32,256]{3,2,1,0:T(8,128)(2,1)}, u32[]{:S(2)}, u32[]{:S(2)}) collective-permute-start(bf16[8,2,32,256]{3,2,1,0:T(8,128)(2,1)} %get-tuple-element.502), channel_id=1, source_target_pairs={{15,0},{14,1},{13,2},{12,3},{7,4},{6,5},{5,6},{4,7},{3,8},{2,9},{1... | collective-permute-start | bytes 786440 | tf_op jit(solution)/shard_map/ppermute | solution.py:34
  377.3 35.1 %collective-permute-start.67 = (bf16[8,2,32,256]{3,2,1,0:T(8,128)(2,1)}, bf16[8,2,32,256]{3,2,1,0:T(8,128)(2,1)}, u32[]{:S(2)}, u32[]{:S(2)}) collective-permute-start(bf16[8,2,32,256]{3,2,1,0:T(8,128)(2,1)} %get-tuple-element.503), channel_id=1, source_target_pairs={{14,0},{15,1},{12,2},{13,3},{6,4},{7,5},{4,6},{5,7},{2,8},{3,9},{0... | collective-permute-start | bytes 786440 | tf_op jit(solution)/shard_map/ppermute | solution.py:34
  377.5 35.6 %collective-permute-start.66 = (bf16[8,2,32,256]{3,2,1,0:T(8,128)(2,1)}, bf16[8,2,32,256]{3,2,1,0:T(8,128)(2,1)}, u32[]{:S(2)}, u32[]{:S(2)}) collective-permute-start(bf16[8,2,32,256]{3,2,1,0:T(8,128)(2,1)} %get-tuple-element.501), channel_id=1, source_target_pairs={{13,0},{12,1},{15,2},{14,3},{5,4},{4,5},{7,6},{6,7},{1,8},{0,9},{3... | collective-permute-start | bytes 786440 | tf_op jit(solution)/shard_map/ppermute | solution.py:34
  412.3 30.2 %collective-permute-start.95 = (bf16[128,256]{1,0:T(8,128)(2,1)}, bf16[128,256]{1,0:T(8,128)(2,1)}, u32[]{:S(2)}, u32[]{:S(2)}) collective-permute-start(bf16[128,256]{1,0:T(8,128)(2,1)} %copy-done.376), channel_id=1, source_target_pairs={{12,4},{4,0},{0,8},{8,16},{16,24},{24,28},{28,20},{20,12},{13,5},{... | collective-permute-start | bytes 196616 | tf_op jit(solution)/shard_map/ppermute | solution.py:52
  413.1 30.6 %collective-permute-start.96 = (bf16[128,256]{1,0:T(8,128)(2,1)}, bf16[128,256]{1,0:T(8,128)(2,1)}, u32[]{:S(2)}, u32[]{:S(2)}) collective-permute-start(bf16[128,256]{1,0:T(8,128)(2,1)} %copy-done.375), channel_id=1, source_target_pairs={{12,20},{4,12},{0,4},{8,0},{16,8},{24,16},{28,24},{20,28},{13,21},... | collective-permute-start | bytes 196616 | tf_op jit(solution)/shard_map/ppermute | solution.py:53
  414.4 30.2 %collective-permute-start.107 = (bf16[128,256]{1,0:T(8,128)(2,1)}, bf16[128,256]{1,0:T(8,128)(2,1)}, u32[]{:S(2)}, u32[]{:S(2)}) collective-permute-start(bf16[128,256]{1,0:T(8,128)(2,1)} %copy-done.374), channel_id=1, source_target_pairs={{12,4},{4,0},{0,8},{8,16},{16,24},{24,28},{28,20},{20,12},{13,5},{... | collective-permute-start | bytes 196616 | tf_op jit(solution)/shard_map/ppermute | solution.py:52
  442.5 27.3 %collective-permute-start.82 = (bf16[128,256]{1,0:T(8,128)(2,1)}, bf16[128,256]{1,0:T(8,128)(2,1)}, u32[]{:S(2)}, u32[]{:S(2)}) collective-permute-start(bf16[128,256]{1,0:T(8,128)(2,1)} %get-tuple-element.302), channel_id=1, source_target_pairs={{12,20},{4,12},{0,4},{8,0},{16,8},{24,16},{28,24},{20,28},{13,21},... | collective-permute-start | bytes 196616 | tf_op jit(solution)/shard_map/ppermute | solution.py:53
  443.7 43.7 %collective-permute-start.93 = (bf16[128,256]{1,0:T(8,128)(2,1)}, bf16[128,256]{1,0:T(8,128)(2,1)}, u32[]{:S(2)}, u32[]{:S(2)}) collective-permute-start(bf16[128,256]{1,0:T(8,128)(2,1)} %get-tuple-element.326), channel_id=1, source_target_pairs={{12,4},{4,0},{0,8},{8,16},{16,24},{24,28},{28,20},{20,12},{13,5},{... | collective-permute-start | bytes 196616 | tf_op jit(solution)/shard_map/ppermute | solution.py:52
  444.5 44.5 %collective-permute-start.94 = (bf16[128,256]{1,0:T(8,128)(2,1)}, bf16[128,256]{1,0:T(8,128)(2,1)}, u32[]{:S(2)}, u32[]{:S(2)}) collective-permute-start(bf16[128,256]{1,0:T(8,128)(2,1)} %get-tuple-element.327), channel_id=1, source_target_pairs={{12,20},{4,12},{0,4},{8,0},{16,8},{24,16},{28,24},{20,28},{13,21},... | collective-permute-start | bytes 196616 | tf_op jit(solution)/shard_map/ppermute | solution.py:53
  489.0 42.1 %collective-permute-start.91 = (bf16[128,256]{1,0:T(8,128)(2,1)}, bf16[128,256]{1,0:T(8,128)(2,1)}, u32[]{:S(2)}, u32[]{:S(2)}) collective-permute-start(bf16[128,256]{1,0:T(8,128)(2,1)} %get-tuple-element.322), channel_id=1, source_target_pairs={{12,4},{4,0},{0,8},{8,16},{16,24},{24,28},{28,20},{20,12},{13,5},{... | collective-permute-start | bytes 196616 | tf_op jit(solution)/shard_map/ppermute | solution.py:52
  489.5 42.5 %collective-permute-start.92 = (bf16[128,256]{1,0:T(8,128)(2,1)}, bf16[128,256]{1,0:T(8,128)(2,1)}, u32[]{:S(2)}, u32[]{:S(2)}) collective-permute-start(bf16[128,256]{1,0:T(8,128)(2,1)} %get-tuple-element.323), channel_id=1, source_target_pairs={{12,20},{4,12},{0,4},{8,0},{16,8},{24,16},{28,24},{20,28},{13,21},... | collective-permute-start | bytes 196616 | tf_op jit(solution)/shard_map/ppermute | solution.py:53
  532.0 40.7 %collective-permute-start.89 = (bf16[128,256]{1,0:T(8,128)(2,1)}, bf16[128,256]{1,0:T(8,128)(2,1)}, u32[]{:S(2)}, u32[]{:S(2)}) collective-permute-start(bf16[128,256]{1,0:T(8,128)(2,1)} %get-tuple-element.318), channel_id=1, source_target_pairs={{12,4},{4,0},{0,8},{8,16},{16,24},{24,28},{28,20},{20,12},{13,5},{... | collective-permute-start | bytes 196616 | tf_op jit(solution)/shard_map/ppermute | solution.py:52
  533.2 40.3 %collective-permute-start.90 = (bf16[128,256]{1,0:T(8,128)(2,1)}, bf16[128,256]{1,0:T(8,128)(2,1)}, u32[]{:S(2)}, u32[]{:S(2)}) collective-permute-start(bf16[128,256]{1,0:T(8,128)(2,1)} %get-tuple-element.319), channel_id=1, source_target_pairs={{12,20},{4,12},{0,4},{8,0},{16,8},{24,16},{28,24},{20,28},{13,21},... | collective-permute-start | bytes 196616 | tf_op jit(solution)/shard_map/ppermute | solution.py:53
  571.4 31.8 %collective-permute-start.87 = (bf16[128,256]{1,0:T(8,128)(2,1)}, bf16[128,256]{1,0:T(8,128)(2,1)S(1)}, u32[]{:S(2)}, u32[]{:S(2)}) collective-permute-start(bf16[128,256]{1,0:T(8,128)(2,1)} %get-tuple-element.314), channel_id=1, source_target_pairs={{12,4},{4,0},{0,8},{8,16},{16,24},{24,28},{28,20},{20,12},{13,5},{... | collective-permute-start | bytes 196616 | tf_op jit(solution)/shard_map/ppermute | solution.py:52
  572.7 32.0 %collective-permute-start.88 = (bf16[128,256]{1,0:T(8,128)(2,1)}, bf16[128,256]{1,0:T(8,128)(2,1)}, u32[]{:S(2)}, u32[]{:S(2)}) collective-permute-start(bf16[128,256]{1,0:T(8,128)(2,1)} %get-tuple-element.315), channel_id=1, source_target_pairs={{12,20},{4,12},{0,4},{8,0},{16,8},{24,16},{28,24},{20,28},{13,21},... | collective-permute-start | bytes 196616 | tf_op jit(solution)/shard_map/ppermute | solution.py:53
  602.6 37.6 %collective-permute-start.169 = (f32[32,512]{1,0:T(8,128)}, f32[32,512]{1,0:T(8,128)}, u32[]{:S(2)}, u32[]{:S(2)}) collective-permute-start(f32[32,512]{1,0:T(8,128)} %get-tuple-element.521), channel_id=1, source_target_pairs={{15,0},{14,1},{13,2},{12,3},{7,4},{6,5},{5,6},{4,7},{3,8},{2,9},{1... | collective-permute-start | bytes 196616 | tf_op jit(solution)/shard_map/ppermute | solution.py:34
  603.9 38.4 %collective-permute-start.168 = (f32[32,512]{1,0:T(8,128)}, f32[32,512]{1,0:T(8,128)}, u32[]{:S(2)}, u32[]{:S(2)}) collective-permute-start(f32[32,512]{1,0:T(8,128)} %get-tuple-element.522), channel_id=1, source_target_pairs={{14,0},{15,1},{12,2},{13,3},{6,4},{7,5},{4,6},{5,7},{2,8},{3,9},{0... | collective-permute-start | bytes 196616 | tf_op jit(solution)/shard_map/ppermute | solution.py:34
  604.8 37.5 %collective-permute-start.167 = (f32[32,512]{1,0:T(8,128)}, f32[32,512]{1,0:T(8,128)}, u32[]{:S(2)}, u32[]{:S(2)}) collective-permute-start(f32[32,512]{1,0:T(8,128)} %get-tuple-element.523), channel_id=1, source_target_pairs={{13,0},{12,1},{15,2},{14,3},{5,4},{4,5},{7,6},{6,7},{1,8},{0,9},{3... | collective-permute-start | bytes 196616 | tf_op jit(solution)/shard_map/ppermute | solution.py:34
  608.4 34.9 %collective-permute-start.166 = (f32[32,512]{1,0:T(8,128)}, f32[32,512]{1,0:T(8,128)}, u32[]{:S(2)}, u32[]{:S(2)}) collective-permute-start(f32[32,512]{1,0:T(8,128)} %get-tuple-element.520), channel_id=1, source_target_pairs={{12,0},{13,1},{14,2},{15,3},{4,4},{5,5},{6,6},{7,7},{0,8},{1,9},{2... | collective-permute-start | bytes 196616 | tf_op jit(solution)/shard_map/ppermute | solution.py:34
  640.2 71.1 %collective-permute-start.170 = (bf16[2,3,128,768]{3,2,1,0:T(8,128)(2,1)}, bf16[2,3,128,768]{3,2,1,0:T(8,128)(2,1)}, u32[]{:S(2)}, u32[]{:S(2)}) collective-permute-start(bf16[2,3,128,768]{3,2,1,0:T(8,128)(2,1)} %pad_maximum_fusion.4), channel_id=1, source_target_pairs={{0,1},{1,0},{2,3},{3,2},{4,5},{5,4},{6,7},{7,6},{8,9},{9,8},{10,11... | collective-permute-start | bytes 3538952 | tf_op jit(solution)/shard_map/ppermute | solution.py:362
  (594 other events, 5101.2 us)
